TPU v7x, 32 devices: a whole 2x2x4 slice. The times are simulated.
32 devices in a mesh: group: 2 (over y), ctx: 4 (over z), smp: 2 (over x), head: 2 (over core).
Axes of the slice: x: 2, y: 2, z: 4, core: 2. Of those that a mesh axis runs over, the one named last changes fastest.
Arguments:
- queries: bfloat16 [512, 2, 4096], P(('group', 'smp'), 'head'), parts along dimension 0, may hold values from -8 to 8
- prefix_cache: bfloat16 [2, 8192, 2, 512], P(None, ('group', 'ctx'), 'head'), parts along dimension 1, may hold values from -8 to 8
- suffix_cache: bfloat16 [2, 512, 128, 2, 512], P(None, ('group', 'ctx', 'smp'), None, 'head'), parts along dimension 1, may hold values from -8 to 8
- suffix_length: int32 [512], P(('group', 'smp')), parts along dimension 0, may hold values from 1 to 128, as said below
- cache_sample: int32 [512], P('group'), parts along dimension 0, may hold values from 0 to 255, as said below
- residual: bfloat16 [512, 8192], P(('group', 'ctx', 'head'), 'smp'), parts along dimension 0, may hold values from -6 to 6
- w_out: bfloat16 [2, 4096, 8192], P('head', 'ctx', 'smp'), may hold values from -0.75 to 0.75
- norm_gain: float32 [8192], P('smp'), may hold values from 0.1 to 1.9
- gate_matrix: bfloat16 [8192, 16384], P('smp', ('ctx', 'head')), may hold values from -0.0625 to 0.0625
- w_up: bfloat16 [8192, 16384], P('smp', ('ctx', 'head')), may hold values from -0.0625 to 0.0625
- w_down: bfloat16 [16384, 8192], P(('ctx', 'head'), 'smp'), may hold values from -0.046875 to 0.046875
Outputs:
- mixed: bfloat16 [512, 8192], P(('group', 'ctx', 'head'), 'smp'), parts along dimension 0
There are 2 independent parts, one for each index of `group`. A program takes and returns all parts, laid end to end along the dimension named above; an argument that names none is the same for every part. Nothing has to cross between parts.
Inputs may be any that keep to these rules, and one draw needn't show every extreme that they name: `suffix_length`: the longest is exactly 128 in every draw. A permutation; cache row r and sample cache_sample[r] lie in the same group, the group of row r being (r // 32) % (2) and that of sample i being i // 128.
All inputs are finite; a program needn't handle non-finite values.
Results may differ from a plain program's by a relative error of at most 0.012.
Values may be sent and summed in bfloat16 or wider, within the bound.
No kernel may reach another device: no remote copies, remote signals or barrier semaphores. Data moves between devices by JAX's collectives and lax.ppermute only.
A program may use at most 192 MiB of HBM per device.

v0:
```python
import jax
import jax.numpy as jnp
from jax import lax
from jax.sharding import PartitionSpec as P

D = 8192
QUERY_HEADS = 64
KEY_VALUE_HEADS = 8
HD = 128


EPSILON = 1e-05


def suffix_piece(row_queries, suffix_cache, row_lengths, key_value_heads_here, score_scale):
    rows_here = suffix_cache.shape[1]
    suffix_keys = suffix_cache[0].reshape(rows_here, -1, key_value_heads_here, HD)
    suffix_values = suffix_cache[1].reshape(rows_here, -1, key_value_heads_here, HD)
    row_scores = (
        jnp.einsum("rjgd,rtjd->rjgt", row_queries, suffix_keys, preferred_element_type=jnp.float32)
        * score_scale
    )
    positions = lax.broadcasted_iota(jnp.int32, row_scores.shape, 3)
    row_scores = jnp.where(positions < row_lengths[:, None, None, None], row_scores, -jnp.inf)
    row_high = jnp.max(row_scores, axis=3)
    row_weights = jnp.exp(row_scores - row_high[..., None])
    row_totals = jnp.sum(row_weights, axis=3)
    row_summed = jnp.einsum(
        "rjgt,rtjd->rjgd",
        row_weights.astype(jnp.bfloat16),
        suffix_values,
        preferred_element_type=jnp.float32,
    )
    row_output = (row_summed / row_totals[..., None]).astype(jnp.bfloat16)
    return (row_output, row_high + jnp.log(row_totals))


def merge_pieces(pieces):
    piece_values, piece_lse = pieces
    item_count = piece_values.shape[0]
    peak = jnp.max(piece_lse, axis=1, keepdims=True)
    piece_weights = jnp.exp(piece_lse - peak)
    shaped = piece_values.reshape(item_count, piece_values.shape[1], piece_lse.shape[2], HD)
    numer = jnp.sum(piece_weights[..., None] * shaped, axis=1)
    denom = jnp.sum(piece_weights, axis=1)
    return (numer / denom[..., None]).reshape(item_count, -1).astype(jnp.bfloat16)


def activate(gate_sum, up_sum, square_sum):
    factor = lax.rsqrt(square_sum / D + EPSILON)[:, None]
    return (jax.nn.silu(factor * gate_sum) * (factor * up_sum)).astype(jnp.bfloat16)


def on_device(
    queries,
    prefix_cache,
    suffix_cache,
    suffix_length,
    cache_sample,
    residual,
    w_out,
    norm_gain,
    gate_matrix,
    w_up,
    w_down,
):
    group_rows = queries.shape[0]
    key_value_heads_here = prefix_cache.shape[3] // HD
    queries_per_key_value = QUERY_HEADS // KEY_VALUE_HEADS
    heads_local = key_value_heads_here * queries_per_key_value
    score_scale = HD ** (-0.5)
    queries_split = queries.reshape(group_rows, key_value_heads_here, queries_per_key_value, HD)
    prefix_keys = prefix_cache[0].reshape(-1, key_value_heads_here, HD)
    prefix_values = prefix_cache[1].reshape(-1, key_value_heads_here, HD)
    scores = (
        jnp.einsum("sjgd,pjd->jsgp", queries_split, prefix_keys, preferred_element_type=jnp.float32)
        * score_scale
    )
    highest = jnp.max(scores, axis=3)
    weights = jnp.exp(scores - highest[..., None])
    totals = jnp.sum(weights, axis=3)
    summed = jnp.einsum(
        "jsgp,pjd->sjgd",
        weights.astype(jnp.bfloat16),
        prefix_values,
        preferred_element_type=jnp.float32,
    )
    prefix_out = (summed / jnp.transpose(totals, (1, 0, 2))[..., None]).astype(jnp.bfloat16)
    prefix_lse = jnp.transpose(highest + jnp.log(totals), (1, 0, 2))
    rows_here = suffix_cache.shape[1]
    flat_index = lax.axis_index("ctx") * lax.axis_size("smp") + lax.axis_index("smp")
    row_ids = lax.dynamic_slice_in_dim(cache_sample, flat_index * rows_here, rows_here, 0)
    local_ids = row_ids % group_rows
    row_queries = jnp.take(queries_split, local_ids, axis=0)
    row_lengths = jnp.take(suffix_length, local_ids, axis=0)
    suffix_out, suffix_lse = suffix_piece(
        row_queries, suffix_cache, row_lengths, key_value_heads_here, score_scale
    )
    onehot = (local_ids[None, :] == jnp.arange(group_rows, dtype=jnp.int32)[:, None]).astype(
        jnp.float32
    )
    present = jnp.sum(onehot, axis=1)[:, None]
    placed_out = jnp.dot(
        onehot,
        suffix_out.reshape(rows_here, -1).astype(jnp.float32),
        precision=lax.Precision.HIGHEST,
    )
    placed_lse = jnp.dot(
        onehot, suffix_lse.reshape(rows_here, heads_local), precision=lax.Precision.HIGHEST
    )
    own_lse = prefix_lse.reshape(group_rows, heads_local)
    other_lse = jnp.where(present > 0, placed_lse, own_lse)
    top = jnp.maximum(own_lse, other_lse)
    own_weight = jnp.exp(own_lse - top)
    other_weight = present * jnp.exp(other_lse - top)
    both_weight = own_weight + other_weight
    own_values = prefix_out.reshape(group_rows, heads_local, HD).astype(jnp.float32)
    other_values = placed_out.reshape(group_rows, heads_local, HD)
    local_out = (
        own_weight[..., None] * own_values + other_weight[..., None] * other_values
    ) / both_weight[..., None]
    local_lse = top + jnp.log(both_weight)
    attn_slice = merge_pieces(
        (
            lax.all_to_all(
                local_out.reshape(group_rows, 1, -1), "ctx", split_axis=2, concat_axis=1, tiled=True
            ),
            lax.all_to_all(
                local_lse.reshape(group_rows, 1, -1), "ctx", split_axis=2, concat_axis=1, tiled=True
            ),
        )
    )
    proj_weight = w_out[0]
    all_attn = lax.all_gather(attn_slice, "smp", axis=0, tiled=True)
    own_state = (
        residual.astype(jnp.float32)
        + lax.psum_scatter(
            jnp.dot(all_attn, proj_weight, preferred_element_type=jnp.float32),
            ("ctx", "head"),
            scatter_dimension=0,
            tiled=True,
        )
    ).astype(jnp.bfloat16)
    state = lax.all_gather(own_state, ("ctx", "head"), axis=0, tiled=True)
    state_wide = state.astype(jnp.float32)
    square_part = jnp.sum(state_wide * state_wide, axis=1)
    scaled = (state_wide * norm_gain).astype(jnp.bfloat16)
    gate_portion = jnp.dot(scaled, gate_matrix, preferred_element_type=jnp.float32)
    up_part = jnp.dot(scaled, w_up, preferred_element_type=jnp.float32)
    gate_sum, up_sum, square_sum = (
        lax.psum(gate_portion.astype(jnp.bfloat16), "smp").astype(jnp.float32),
        lax.psum(up_part.astype(jnp.bfloat16), "smp").astype(jnp.float32),
        lax.psum(square_part.astype(jnp.bfloat16), "smp").astype(jnp.float32),
    )
    activated = activate(gate_sum, up_sum, square_sum)
    ffn_rows = lax.psum_scatter(
        jnp.dot(activated, w_down, preferred_element_type=jnp.float32).astype(jnp.bfloat16),
        ("ctx", "head"),
        scatter_dimension=0,
        tiled=True,
    ).astype(jnp.float32)
    return (own_state.astype(jnp.float32) + ffn_rows).astype(jnp.bfloat16)


def solution(mesh):
    in_specs = (
        P(("group", "smp"), "head", None),
        P(None, ("group", "ctx"), "head", None),
        P(None, ("group", "ctx", "smp"), None, "head", None),
        P(("group", "smp")),
        P("group"),
        P(("group", "ctx", "head"), "smp"),
        P("head", "ctx", "smp"),
        P("smp"),
        P("smp", ("ctx", "head")),
        P("smp", ("ctx", "head")),
        P(("ctx", "head"), "smp"),
    )
    out_specs = P(("group", "ctx", "head"), "smp")
    return jax.shard_map(
        on_device, mesh=mesh, in_specs=in_specs, out_specs=out_specs, check_vma=False
    )
```

profile of v0, /device:TPU:0, one launch (start us, length us, event | category | flops | bytes accessed | tf_op | source)
XLA Modules:
  0.0 359.7 jit_solution(7161917489603728494)
XLA Ops:
  10.4 5.9 %fusion.46 = (bf16[1,32,128,1,512]{4,2,3,1,0:T(8,128)(2,1)}, bf16[1,32,128,1,512]{4,2,3,1,0:T(8,128)(2,1)}) fusion(bf16[2,32,128,1,512]{4,2,3,1,0:T(8,128)(2,1)} %param.13), kind=kLoop, calls=%fused_computation.77 | loop fusion | bytes 16777216 | tf_op jit(solution)/shard_map/slice | solution.py:18
  16.4 6.4 %copy.57 = bf16[1,32,128,1,512]{2,4,1,3,0:T(8,128)(2,1)} copy(bf16[1,32,128,1,512]{4,2,3,1,0:T(8,128)(2,1)} %get-tuple-element.18) | data formatting | bytes 8388608
  22.8 8.1 %multiply_reduce_fusion = (f32[4,128,8]{1,2,0:T(8,128)S(1)}, f32[4,128,8,1024]{3,1,2,0:T(8,128)}) fusion(bf16[1024,4,128,1]{0,2,3,1:T(8,128)(2,1)S(1)} %bitcast.92, bf16[128,4,8,128]{3,2,1,0:T(8,128)(2,1)S(1)} %bitcast.89), kind=kOutput, calls=%fused_computation.3 | convolution fusion | flops 1082126336 | bytes 18890752 | tf_op jit(solution)/shard_map/sjgd,pjd->jsgp/dot_general | solution.py:76
  32.2 3.5 fusion.48
  36.4 7.7 %fusion.1 = f32[4,128,8]{1,2,0:T(8,128)S(1)} fusion(f32[4,128,8,1024]{3,1,2,0:T(8,128)} %get-tuple-element.22, f32[4,128,8]{1,2,0:T(8,128)S(1)} %get-tuple-element.21), kind=kLoop, calls=%fused_computation.5 | loop fusion | flops 12578816 | bytes 16809984 | tf_op jit(solution)/shard_map/reduce_sum | solution.py:81
  44.9 6.3 %all-to-all-start = ((f32[128,1,32]{0,1,2:T(1,128)}), f32[128,1,32]{0,1,2:T(1,128)S(1)}, u32[]{:S(2)}, u32[]{:S(2)}) async-start(f32[128,1,32]{0,1,2:T(1,128)} %bitcast.8), calls=%async_computation | async-start | bytes 32768 | tf_op jit(solution)/shard_map/all_to_all | solution.py:128
  51.7 6.4 %copy.58 = bf16[1,32,128,1,512]{2,4,1,3,0:T(8,128)(2,1)} copy(bf16[1,32,128,1,512]{4,2,3,1,0:T(8,128)(2,1)} %get-tuple-element.17) | data formatting | bytes 8388608
  58.1 4.5 %fusion.18 = bf16[32,4,8,128]{3,2,1,0:T(8,128)(2,1)S(1)} fusion(bf16[32,128,4,128]{1,3,2,0:T(8,128)(2,1)} %bitcast.91, f32[32,4,8,128]{3,2,1,0:T(8,128)S(1)} %get-tuple-element.24, f32[32,4,8]{2,1,0:T(4,128)S(1)} %fusion.24, f32[32,4,8]{2,1,0:T(4,128)S(1)} %get-tuple-element.23), kind=kOutput, calls=%fused_computation.28 | convolution fusion | flops 34078720 | bytes 4988928 | tf_op jit(solution)/shard_map/rjgt,rtjd->rjgd/dot_general | solution.py:28
  62.7 7.6 %fusion.12 = bf16[128,4,8,128]{0,3,2,1:T(8,128)(2,1)S(1)} fusion(bf16[1024,4,128,1]{0,2,3,1:T(8,128)(2,1)S(1)} %bitcast.96, f32[4,128,8,1024]{3,1,2,0:T(8,128)} %get-tuple-element.22, f32[4,128,8]{1,2,0:T(8,128)S(1)} %get-tuple-element.21, f32[128,4,8]{0,2,1:T(8,128)S(1)} %bitcast.99), kind=kOutput, calls=%fused_computation.22 | convolution fusion | flops 1087373312 | bytes 18907136 | tf_op jit(solution)/shard_map/jsgp,pjd->sjgd/dot_general | solution.py:82
  70.3 2.0 fusion.11
  72.3 5.1 %all-to-all-start.1 = ((f32[128,1,4096]{0,1,2:T(1,128)}), f32[128,1,4096]{0,1,2:T(1,128)S(1)}, u32[]{:S(2)}, u32[]{:S(2)}) async-start(f32[128,1,4096]{0,1,2:T(1,128)} %bitcast.93), calls=%async_computation.1 | async-start | bytes 4194304 | tf_op jit(solution)/shard_map/all_to_all | solution.py:125
  77.5 47.6 %all-to-all-done.1 = f32[128,1,4096]{0,1,2:T(1,128)S(1)} async-done(((f32[128,1,4096]{0,1,2:T(1,128)}), f32[128,1,4096]{0,1,2:T(1,128)S(1)}, u32[]{:S(2)}, u32[]{:S(2)}) %all-to-all-start.1) | async-done | bytes 2097184 | tf_op jit(solution)/shard_map/all_to_all | solution.py:125
  125.3 8.1 %all_gather.6 = bf16[256,1024]{0,1:T(8,128)(2,1)S(1)} all-gather(bf16[128,1024]{0,1:T(8,128)(2,1)S(1)} %bitcast.94), channel_id=1, replica_groups=mesh['group'=2,'ctx'=4,'smp'=2,'head'=2] {'smp'}, dimensions={0}, use_global_device_ids=true | all-gather | bytes 786432 | tf_op jit(solution)/shard_map/all_gather | solution.py:134
  133.5 7.7 %fusion.4 = f32[256,4096]{1,0:T(8,128)} fusion(bf16[256,1024]{0,1:T(8,128)(2,1)S(1)} %all_gather.6, bf16[1,1024,4096]{2,1,0:T(8,128)(2,1)} %param.17), kind=kOutput, calls=%fused_computation.7 | convolution fusion | flops 2147483648 | bytes 13107200 | tf_op jit(solution)/shard_map/dot_general | solution.py:138
  141.3 48.3 %reduce-scatter.3.cloned.1.call-done = f32[32,4096]{1,0:T(8,128)} async-done(((f32[256,4096]{1,0:T(8,128)}), f32[32,4096]{1,0:T(8,128)}) %reduce-scatter.3.cloned.1.call-update) | async-done | bytes 524304 | tf_op jit(solution)/shard_map/reduce_scatter | solution.py:137
  189.6 1.8 add_convert_fusion.1
  191.5 27.4 %all-gather.2.cloned.1.call-done = bf16[256,4096]{1,0:T(8,128)(2,1)} async-done(((bf16[32,4096]{1,0:T(8,128)(2,1)}), bf16[256,4096]{1,0:T(8,128)(2,1)}) %all-gather.2.cloned.1.call-update) | async-done | bytes 2097168 | tf_op jit(solution)/shard_map/all_gather | solution.py:144
  218.8 12.0 %convolution_convert_fusion.1 = bf16[256,2048]{1,0:T(8,128)(2,1)} fusion(bf16[4096,2048]{1,0:T(8,128)(2,1)} %param.20, bf16[256,4096]{1,0:T(8,128)(2,1)} %all-gather.2.cloned.1.call-done, f32[4096]{0:T(1024)S(1)} %copy-done.6), kind=kOutput, calls=%fused_computation.16 | convolution fusion | flops 4298637312 | bytes 19939328 | tf_op jit(solution)/shard_map/dot_general | solution.py:149
  230.9 9.3 %convolution_convert_fusion.2 = bf16[256,2048]{1,0:T(8,128)(2,1)} fusion(bf16[4096,2048]{1,0:T(8,128)(2,1)} %param.19, bf16[256,4096]{1,0:T(8,128)(2,1)S(1)} %copy-done.3, f32[4096]{0:T(1024)S(1)} %copy-done.6), kind=kOutput, calls=%fused_computation.17 | convolution fusion | flops 4298637312 | bytes 19939328 | tf_op jit(solution)/shard_map/dot_general | solution.py:148
  240.7 5.2 %psum.21 = bf16[256]{0:T(256)(128)(2,1)S(1)} all-reduce(bf16[256]{0:T(256)(128)(2,1)S(1)} %fusion.8), channel_id=1, replica_groups=mesh['group'=2,'ctx'=4,'smp'=2,'head'=2] {'smp'}, use_global_device_ids=true, to_apply=%region_10.11 | all-reduce | flops 256 | bytes 1024 | tf_op jit(solution)/shard_map/psum | solution.py:153
  245.9 57.0 %all-reduce.3.cloned.1.call-done = (bf16[256,2048]{1,0:T(8,128)(2,1)}, bf16[256,2048]{1,0:T(8,128)(2,1)}) async-done(((bf16[256,2048]{1,0:T(8,128)(2,1)}, bf16[256,2048]{1,0:T(8,128)(2,1)}), (bf16[256,2048]{1,0:T(8,128)(2,1)}, bf16[256,2048]{1,0:T(8,128)(2,1)})) %all-reduce.3.cloned.1.call-update) | async-done | bytes 2097168 | tf_op jit(solution)/shard_map/psum | solution.py:152
  302.9 12.6 %convolution_convert_fusion = bf16[256,4096]{1,0:T(8,128)(2,1)} fusion(bf16[2048,4096]{1,0:T(8,128)(2,1)} %param.21, bf16[256,2048]{1,0:T(8,128)(2,1)} %get-tuple-element.5, bf16[256,2048]{1,0:T(8,128)(2,1)} %get-tuple-element.6, f32[256]{0:T(256)S(1)} %add_rsqrt_fusion), kind=kOutput, calls=%fused_computation.13 | convolution fusion | flops 4301258752 | bytes 20972544 | tf_op jit(solution)/shard_map/dot_general | solution.py:157
  315.5 35.9 %reduce-scatter.5.cloned.1.call-done = bf16[32,4096]{1,0:T(8,128)(2,1)} async-done(((bf16[256,4096]{1,0:T(8,128)(2,1)}), bf16[32,4096]{1,0:T(8,128)(2,1)}) %reduce-scatter.5.cloned.1.call-update) | async-done | bytes 262160 | tf_op jit(solution)/shard_map/reduce_scatter | solution.py:156
  351.4 1.7 add_convert_fusion
  (44 shorter events, 8.2 us)
Async XLA Ops:
  6.5 25.0 %copy-start = (s32[128]{0:T(128)S(1)}, s32[128]{0:T(128)}, u32[]{:S(2)}) copy-start(s32[128]{0:T(128)} %param.14) | copy-start | bytes 1540
  6.5 3.7 %copy-start.5 = (s32[256]{0:T(256)S(1)}, s32[256]{0:T(256)}, u32[]{:S(2)}) copy-start(s32[256]{0:T(256)} %param.15) | copy-start | bytes 3076
  44.9 27.5 %all-to-all-start = ((f32[128,1,32]{0,1,2:T(1,128)}), f32[128,1,32]{0,1,2:T(1,128)S(1)}, u32[]{:S(2)}, u32[]{:S(2)}) async-start(f32[128,1,32]{0,1,2:T(1,128)} %bitcast.8), calls=%async_computation | async-start | bytes 32768 | tf_op jit(solution)/shard_map/all_to_all | solution.py:128
  72.3 52.7 %all-to-all-start.1 = ((f32[128,1,4096]{0,1,2:T(1,128)}), f32[128,1,4096]{0,1,2:T(1,128)S(1)}, u32[]{:S(2)}, u32[]{:S(2)}) async-start(f32[128,1,4096]{0,1,2:T(1,128)} %bitcast.93), calls=%async_computation.1 | async-start | bytes 4194304 | tf_op jit(solution)/shard_map/all_to_all | solution.py:125
  77.4 112.2 %reduce-scatter.3.cloned.1.call-start = ((), (), s32[]{:S(2)}) async-start(), calls=%async_computation.4 | async-start | bytes 4718592 | tf_op jit(solution)/shard_map/reduce_scatter | solution.py:137
  141.2 48.4 %copy-start.4 = (bf16[32,4096]{1,0:T(8,128)(2,1)S(1)}, bf16[32,4096]{1,0:T(8,128)(2,1)}, u32[]{:S(2)}) copy-start(bf16[32,4096]{1,0:T(8,128)(2,1)} %param.16) | copy-start | bytes 786436
  141.2 77.7 %copy-start.6 = (f32[4096]{0:T(1024)S(1)}, f32[4096]{0:T(1024)}, u32[]{:S(2)}) copy-start(f32[4096]{0:T(1024)} %param.18) | copy-start | bytes 49156
  141.2 77.6 %all-gather.2.cloned.1.call-start = ((), (), s32[]{:S(2)}) async-start(), calls=%async_computation.5 | async-start | bytes 2359296 | tf_op jit(solution)/shard_map/all_gather | solution.py:144
  191.4 111.5 %all-reduce.3.cloned.1.call-start = ((), (), s32[]{:S(2)}) async-start(), calls=%async_computation.7 | async-start | bytes 4194304 | tf_op jit(solution)/shard_map/psum | solution.py:152
  218.8 12.0 %copy-start.3 = (bf16[256,4096]{1,0:T(8,128)(2,1)S(1)}, bf16[256,4096]{1,0:T(8,128)(2,1)}, u32[]{:S(2)}) copy-start(bf16[256,4096]{1,0:T(8,128)(2,1)} %all-gather.2.cloned.1.call-done) | copy-start | bytes 6291460
  240.2 111.3 %reduce-scatter.5.cloned.1.call-start = ((), (), s32[]{:S(2)}) async-start(), calls=%async_computation.6 | async-start | bytes 2359296 | tf_op jit(solution)/shard_map/reduce_scatter | solution.py:156
  302.9 48.5 %copy-start.2 = (bf16[32,4096]{1,0:T(8,128)(2,1)S(1)}, bf16[32,4096]{1,0:T(8,128)(2,1)}, u32[]{:S(2)}) copy-start(bf16[32,4096]{1,0:T(8,128)(2,1)} %add_convert_fusion.1) | copy-start | bytes 786436
  302.9 50.3 %copy-start.1 = (s32[128]{0:T(128)S(1)}, s32[128]{0:T(128)}, u32[]{:S(2)}) copy-start(s32[128]{0:T(128)} %param.14) | copy-start | bytes 1540
Sparse Core Ops, SparseCore 0:
  141.3 48.2 reduce-scatter.2
  191.5 27.2 all-gather.1
  240.3 62.5 all-reduce.2
  315.6 35.7 reduce-scatter.4
where the time goes:
time: 361 us; the launch traced here: 360 us
  waiting for transfers between devices  216 us (60%)
  matrix products  68.3 us (19%)
  local copies, waits for them, and re-layouts  24.4 us (7%)
  blocking collectives  13.3 us (4%)
  between operations  13.2 us (4%)
  other arithmetic  12.6 us (3%)
  starting transfers between devices  11.5 us (3%)
    psum x1, waiting for transfers between devices, on_device(): lax.psum(up_part.astype(jnp.bfloat16), 'smp').astype(jnp.float32)  57 us
    reduce_scatter x1, waiting for transfers between devices, on_device(): lax.psum_scatter(jnp.dot(all_attn, proj_weight, preferred_element_type=jn...  48.3 us
    all_to_all x1, waiting for transfers between devices, on_device(): lax.all_to_all(local_out.reshape(group_rows, 1, -1), 'ctx', split_axis=2,...  47.6 us
    reduce_scatter x1, waiting for transfers between devices, on_device(): lax.psum_scatter(jnp.dot(activated, w_down, preferred_element_type=jnp.fl...  35.9 us
    all_gather x1, waiting for transfers between devices, on_device(): state = lax.all_gather(own_state, ('ctx', 'head'), axis=0, tiled=True)  27.4 us
    unnamed x18, local copies, waits for them, and re-layouts  14.8 us
    dot_general x1, matrix products, on_device(): jnp.dot(activated, w_down, preferred_element_type=jnp.float32)  12.6 us
    dot_general x1, matrix products, on_device(): up_part = jnp.dot(scaled, w_up, preferred_element_type=jnp.float32)  12 us
  transfers between devices with their start and end apart: 6, of which 5 were waited for; matrix products, arithmetic and copies ran while one was open for 6% of the time, Pallas kernels for 0%

commit v1 on v0

v1 whole, which is shorter than its diff:
```python
import functools

import jax
import jax.numpy as jnp
from jax import lax
from jax.experimental import pallas as pl
from jax.experimental.pallas import tpu as pltpu
from jax.sharding import PartitionSpec as P

D = 8192
QUERY_HEADS = 64
KEY_VALUE_HEADS = 8
HD = 128
EPSILON = 1e-05

BF16 = jnp.bfloat16
F32 = jnp.float32
VMEM_LIMIT = 48 * 1024 * 1024
STAT_ROWS = 32
LOG2E = 1.4426950408889634
LN2 = 0.6931471805599453


def params(**more):
    return pltpu.CompilerParams(vmem_limit_bytes=VMEM_LIMIT, **more)


def dot(a, b):
    return jnp.dot(a, b, preferred_element_type=F32)


def dot_nt(a, b):
    return lax.dot_general(a, b, (((1,), (1,)), ((), ())), preferred_element_type=F32)


def split3(x):
    hi = x.astype(BF16).astype(F32)
    mid = (x - hi).astype(BF16).astype(F32)
    low = (x - hi - mid).astype(BF16).astype(F32)
    return hi, mid, low


def shift(x, axis, size, k):
    return lax.ppermute(x, axis, [(i, (i + k) % size) for i in range(size)])


def attention_kernel(
    heads, chunk_ref, ids_ref, lens_ref, q_ref, pk_ref, pv_ref, sk_ref, sv_ref, msg_ref
):
    samples = q_ref.shape[0]
    rows, span = sk_ref.shape[1], sk_ref.shape[2]
    lanes_s = rows * heads
    scale2 = HD**-0.5 * LOG2E
    queries = jnp.concatenate(
        [q_ref[:, g * HD : (g + 1) * HD] for g in range(heads)], axis=0
    )

    shape = (lanes_s, heads * samples)
    lane = lax.broadcasted_iota(jnp.int32, shape, 1)
    row = lax.broadcasted_iota(jnp.int32, shape, 0)
    wanted = ids_ref[...] + lax.rem(row, heads) * samples
    pick = jnp.where(lane == wanted, 1.0, 0.0).astype(BF16)
    row_queries = dot(pick, queries)

    per_tile = min(rows, max(1, 128 // heads))
    width = per_tile * heads
    outs, lses = [], []
    for tile in range(rows // per_tile):
        at = tile * per_tile
        q_tile = row_queries[at * heads : at * heads + width]
        own = lax.broadcasted_iota(jnp.int32, (width, HD), 0) // heads
        q_wide = jnp.concatenate(
            [jnp.where(own == r, q_tile, 0.0).astype(BF16) for r in range(per_tile)], axis=1
        )
        keys = jnp.concatenate([sk_ref[0, at + r] for r in range(per_tile)], axis=1)
        s = dot_nt(keys, q_wide) * scale2
        t = lax.broadcasted_iota(jnp.int32, s.shape, 0)
        s = jnp.where(t < lens_ref[:, at * heads : at * heads + width], s, -jnp.inf)
        high = jnp.max(s, axis=0, keepdims=True)
        weights = jnp.exp2(s - high)
        total = jnp.sum(weights, axis=0, keepdims=True)
        turned = weights.T
        own_t = lax.broadcasted_iota(jnp.int32, (width, span), 0) // heads
        w_wide = jnp.concatenate(
            [jnp.where(own_t == r, turned, 0.0).astype(BF16) for r in range(per_tile)], axis=1
        )
        values = sv_ref[0, at : at + per_tile].reshape(per_tile * span, HD)
        out = dot(w_wide, values).T / total
        outs.append(out)
        lses.append(high + jnp.log2(total))
    lse_s = jnp.concatenate(lses, axis=1)
    hi, mid, low = split3(lse_s)
    sub = lax.broadcasted_iota(jnp.int32, (16, lanes_s), 0)
    stats = jnp.where(sub == 0, hi, jnp.where(sub == 1, mid, jnp.where(sub == 2, low, 1.0)))
    to_place = jnp.concatenate([jnp.concatenate(outs, axis=1), stats], axis=0).astype(BF16)
    placed = dot(to_place, pick)
    placed_lse = placed[HD : HD + 1] + placed[HD + 1 : HD + 2] + placed[HD + 2 : HD + 3]
    present = placed[HD + 3 : HD + 4]

    keys = pk_ref[0]
    values_t = pv_ref[0].T
    rows_out = []
    for g in range(heads):
        at = slice(g * samples, (g + 1) * samples)
        s = dot_nt(keys, queries[at])
        high = jnp.max(s, axis=0, keepdims=True) * scale2
        weights = jnp.exp2(s * scale2 - high)
        total = jnp.sum(weights, axis=0, keepdims=True)
        out = dot(values_t, weights.astype(BF16))
        here = present[:, at] > 0.5
        other = jnp.where(here, placed_lse[:, at], high)
        top = jnp.maximum(high, other)
        own_weight = jnp.exp2(high - top)
        other_weight = jnp.where(here, jnp.exp2(other - top), 0.0)
        both = own_weight * total + other_weight
        out = (out * own_weight + placed[:HD, at] * other_weight) / both
        msg_ref[g * HD : (g + 1) * HD, :] = out.astype(BF16)
        rows_out.append(top + jnp.log2(both))
    sub = lax.broadcasted_iota(jnp.int32, (STAT_ROWS, samples), 0)
    stats = jnp.zeros((STAT_ROWS, samples), F32)
    for g in range(heads):
        for part, value in enumerate(split3(rows_out[g])):
            stats = jnp.where(sub == part * heads + g, value, stats)
    msg_ref[heads * HD :, :] = stats.astype(BF16)


def attention_piece(chunk, kv, ids, lens, queries, prefix, suffix, heads):
    samples = queries.shape[0]
    block, rows, span = prefix.shape[1], suffix.shape[1], suffix.shape[2]
    out_rows = heads * HD + STAT_ROWS
    spec = pltpu.PrefetchScalarGridSpec(
        num_scalar_prefetch=1,
        grid=(1,),
        in_specs=[
            pl.BlockSpec(ids.shape, lambda i, c: (0, 0)),
            pl.BlockSpec(lens.shape, lambda i, c: (0, 0)),
            pl.BlockSpec((samples, heads * HD), lambda i, c: (0, c[0])),
            pl.BlockSpec((1, block, HD), lambda i, c: (0, 0, c[1])),
            pl.BlockSpec((1, block, HD), lambda i, c: (1, 0, c[1])),
            pl.BlockSpec((1, rows, span, HD), lambda i, c: (0, 0, 0, c[1])),
            pl.BlockSpec((1, rows, span, HD), lambda i, c: (1, 0, 0, c[1])),
        ],
        out_specs=pl.BlockSpec((out_rows, samples), lambda i, c: (0, 0)),
    )
    return pl.pallas_call(
        functools.partial(attention_kernel, heads),
        grid_spec=spec,
        out_shape=jax.ShapeDtypeStruct((out_rows, samples), BF16),
        compiler_params=params(),
        cost_estimate=pl.CostEstimate(
            flops=4 * samples * heads * block * HD * 4,
            bytes_accessed=2 * (2 * block + 2 * rows * span) * HD * 2,
            transcendentals=samples * heads * block,
        ),
    )(jnp.stack([chunk, kv]), ids, lens, queries, prefix, prefix, suffix, suffix)


def merge_kernel(heads, *refs):
    pieces, out_ref = refs[:-1], refs[-1]
    top_rows = heads * HD
    lses = []
    for ref in pieces:
        stats = ref[top_rows:, :].astype(F32)
        lses.append(
            stats[:heads] + stats[heads : 2 * heads] + stats[2 * heads : 3 * heads]
        )
    top = functools.reduce(jnp.maximum, lses)
    weights = [jnp.exp2(lse - top) for lse in lses]
    denom = functools.reduce(jnp.add, weights)
    weights = [w / denom for w in weights]
    for g in range(heads):
        total = None
        for ref, w in zip(pieces, weights):
            term = ref[g * HD : (g + 1) * HD, :].astype(F32) * w[g : g + 1]
            total = term if total is None else total + term
        out_ref[:, g * HD : (g + 1) * HD] = total.T.astype(BF16)


def merge(pieces, heads):
    samples = pieces[0].shape[1]
    return pl.pallas_call(
        functools.partial(merge_kernel, heads),
        out_shape=jax.ShapeDtypeStruct((samples, heads * HD), BF16),
        compiler_params=params(),
        cost_estimate=pl.CostEstimate(
            flops=2 * len(pieces) * samples * heads * HD,
            bytes_accessed=2 * (len(pieces) + 1) * samples * heads * HD,
            transcendentals=0,
        ),
    )(*pieces)


def proj_kernel(n_ctx, n_head, own_rows, n_smp, where_ref, *refs):
    attn_refs = refs[:n_smp]
    w_ref, keep_ref, *send_refs, full, lhs = refs[n_smp:]
    ctx, smp, head = where_ref[0], where_ref[1], where_ref[2]
    samples = attn_refs[0].shape[0]

    @pl.when(pl.program_id(0) == 0)
    def _():
        for k, ref in enumerate(attn_refs):
            at = lax.rem(smp + n_smp - k, n_smp) * samples
            full[pl.ds(pl.multiple_of(at, 16), samples), :] = ref[...]
        for b in range(n_head):
            h = lax.rem(head + b, n_head)
            for t in range(n_ctx):
                c = lax.rem(ctx + n_ctx - t, n_ctx)
                at = (c * n_head + h) * own_rows
                to = (b * n_ctx + t) * own_rows
                lhs[to : to + own_rows, :] = full[
                    pl.ds(pl.multiple_of(at, 16), own_rows), :
                ]

    out = dot(lhs[...], w_ref[0]).astype(BF16)
    per = n_ctx * own_rows
    keep_ref[...] = out[:per]
    for b, ref in enumerate(send_refs):
        ref[...] = out[(b + 1) * per : (b + 2) * per]


def project(where, attn, w_out, n_ctx, n_head, own_rows):
    n_smp = len(attn)
    samples, depth = attn[0].shape
    width = w_out.shape[2]
    tile = min(512, width)
    per = n_ctx * own_rows
    rows = per * n_head
    spec = pltpu.PrefetchScalarGridSpec(
        num_scalar_prefetch=1,
        grid=(width // tile,),
        in_specs=[pl.BlockSpec((samples, depth), lambda i, w: (0, 0))] * n_smp
        + [pl.BlockSpec((1, depth, tile), lambda i, w: (0, 0, i))],
        out_specs=[pl.BlockSpec((per, tile), lambda i, w: (0, i))] * n_head,
        scratch_shapes=[
            pltpu.VMEM((n_smp * samples, depth), BF16),
            pltpu.VMEM((rows, depth), BF16),
        ],
    )
    return pl.pallas_call(
        functools.partial(proj_kernel, n_ctx, n_head, own_rows, n_smp),
        grid_spec=spec,
        out_shape=[jax.ShapeDtypeStruct((per, width), BF16)] * n_head,
        compiler_params=params(),
        cost_estimate=pl.CostEstimate(
            flops=2 * rows * depth * width,
            bytes_accessed=2 * (depth * width + rows * depth + rows * width),
            transcendentals=0,
        ),
    )(where, *attn, w_out)


def exchange_heads(parts, n_head):
    total = parts[0].astype(F32)
    for b in range(1, n_head):
        total = total + shift(parts[b], "head", n_head, b).astype(F32)
    return total.astype(BF16)


def ring_sum(x, n_ctx, own_rows):
    width = x.shape[1]
    half = width // 2

    def part(t, side):
        return x[t * own_rows : (t + 1) * own_rows, side * half : (side + 1) * half]

    running = [None, None]
    for step in range(1, n_ctx):
        for side in range(2):
            t = step if side == 0 else n_ctx - step
            mine = part(t, side)
            if running[side] is not None:
                mine = (running[side].astype(F32) + mine.astype(F32)).astype(BF16)
            running[side] = shift(mine, "ctx", n_ctx, 1 if side == 0 else -1)
    return running


def state_kernel(a_ref, b_ref, own_ref, res_ref, gain_ref, state_ref, ma_ref, mb_ref):
    half = a_ref.shape[1]
    square = None
    for side, ref in enumerate((a_ref, b_ref)):
        at = slice(side * half, (side + 1) * half)
        total = (
            res_ref[:, at].astype(F32) + own_ref[:, at].astype(F32) + ref[...].astype(F32)
        )
        state = total.astype(BF16)
        state_ref[:, at] = state
        wide = state.astype(F32)
        scaled = (wide * gain_ref[:, at]).astype(BF16)
        if side == 0:
            ma_ref[...] = scaled
        else:
            mb_ref[:, :half] = scaled
        part = jnp.sum(wide * wide, axis=1, keepdims=True)
        square = part if square is None else square + part
    hi, mid, low = split3(square)
    lane = lax.broadcasted_iota(jnp.int32, (square.shape[0], HD), 1)
    stats = jnp.where(
        lane == 0, hi, jnp.where(lane == 1, mid, jnp.where(lane == 2, low, 0.0))
    )
    mb_ref[:, half:] = stats.astype(BF16)


def make_state(halves, own, residual, gain):
    rows, width = residual.shape
    return pl.pallas_call(
        state_kernel,
        out_shape=[
            jax.ShapeDtypeStruct((rows, width), BF16),
            jax.ShapeDtypeStruct((rows, width // 2), BF16),
            jax.ShapeDtypeStruct((rows, width // 2 + HD), BF16),
        ],
        compiler_params=params(),
    )(*halves, own, residual, gain)


def ring_gather(a, b, n_ctx):
    got_a, got_b = [a], [b]
    for _ in range(1, n_ctx):
        got_a.append(shift(got_a[-1], "ctx", n_ctx, 1))
        got_b.append(shift(got_b[-1], "ctx", n_ctx, -1))
    return got_a, [got_b[(n_ctx - t) % n_ctx] for t in range(n_ctx)]


def gate_up_kernel(where_ref, x_ref, g_ref, u_ref, out_ref, g_acc, u_acc):
    k = pl.program_id(0)
    x = x_ref[...]
    gate = dot(x, g_ref[...])
    up = dot(x, u_ref[...])

    @pl.when(k == 0)
    def _():
        g_acc[...] = gate
        u_acc[...] = up

    @pl.when(k > 0)
    def _():
        g_acc[...] += gate
        u_acc[...] += up

    @pl.when(k == pl.num_programs(0) - 1)
    def _():
        width = g_acc.shape[1]
        out_ref[:, :width] = g_acc[...].astype(out_ref.dtype)
        out_ref[:, width:] = u_acc[...].astype(out_ref.dtype)


def gate_up(block, x, gate_matrix, w_up, units, dtype):
    rows, depth = x.shape[0], gate_matrix.shape[0]
    tile = min(512, depth)
    spec = pltpu.PrefetchScalarGridSpec(
        num_scalar_prefetch=1,
        grid=(depth // tile,),
        in_specs=[
            pl.BlockSpec((rows, tile), lambda k, w: (0, k)),
            pl.BlockSpec((tile, units), lambda k, w: (k, w[0])),
            pl.BlockSpec((tile, units), lambda k, w: (k, w[0])),
        ],
        out_specs=pl.BlockSpec((rows, 2 * units), lambda k, w: (0, 0)),
        scratch_shapes=[pltpu.VMEM((rows, units), F32)] * 2,
    )
    return pl.pallas_call(
        gate_up_kernel,
        grid_spec=spec,
        out_shape=jax.ShapeDtypeStruct((rows, 2 * units), dtype),
        compiler_params=params(),
        cost_estimate=pl.CostEstimate(
            flops=4 * rows * depth * units,
            bytes_accessed=2 * (2 * depth * units + rows * depth + 2 * rows * units),
            transcendentals=0,
        ),
    )(block.reshape(1), x, gate_matrix, w_up)


def act_kernel(n_recv, n_sq, *refs):
    own_ref, refs = refs[0], refs[1:]
    recv, squares, out_ref = refs[:n_recv], refs[n_recv : n_recv + n_sq], refs[-1]
    total = own_ref[...].astype(F32)
    for ref in recv:
        total = total + ref[...].astype(F32)
    square = functools.reduce(jnp.add, [ref[...].astype(F32) for ref in squares])
    factor = lax.rsqrt(jnp.sum(square, axis=1, keepdims=True) / D + EPSILON)
    units = out_ref.shape[1]
    gate = factor * total[:, :units]
    up = factor * total[:, units:]
    out_ref[...] = (gate / (1.0 + jnp.exp(-gate)) * up).astype(BF16)


def activate(own, recv, squares, units):
    rows = own.shape[0]
    return pl.pallas_call(
        functools.partial(act_kernel, len(recv), len(squares)),
        out_shape=jax.ShapeDtypeStruct((rows, units), BF16),
        compiler_params=params(),
    )(own, *recv, *squares)


def down_kernel(n_parts, has_acc, n_head, where_ref, *refs):
    xs = refs[:n_parts]
    w_refs = refs[n_parts : 2 * n_parts]
    refs = refs[2 * n_parts :]
    total = None
    for x_ref, w_ref in zip(xs, w_refs):
        term = dot(x_ref[...], w_ref[...])
        total = term if total is None else total + term
    if has_acc:
        acc_ref, *outs = refs
        total = total + acc_ref[...]
        per = total.shape[0] // n_head
        for b, ref in enumerate(outs):
            ref[...] = total[b * per : (b + 1) * per].astype(BF16)
    else:
        refs[0][...] = total


def down(blocks, xs, w_down, acc, n_head):
    rows, units = xs[0].shape
    width = w_down.shape[1]
    tile = min(512, width)
    n = len(xs)

    def w_spec(i):
        return pl.BlockSpec((units, tile), lambda k, w: (w[i], k))

    in_specs = [pl.BlockSpec((rows, units), lambda k, w: (0, 0))] * n
    in_specs += [w_spec(i) for i in range(n)]
    args = [*xs, *([w_down] * n)]
    if acc is not None:
        in_specs.append(pl.BlockSpec((rows, tile), lambda k, w: (0, k)))
        args.append(acc)
        per = rows // n_head
        out_shape = [jax.ShapeDtypeStruct((per, width), BF16)] * n_head
        out_specs = [pl.BlockSpec((per, tile), lambda k, w: (0, k))] * n_head
    else:
        out_shape = jax.ShapeDtypeStruct((rows, width), F32)
        out_specs = pl.BlockSpec((rows, tile), lambda k, w: (0, k))
    return pl.pallas_call(
        functools.partial(down_kernel, n, acc is not None, n_head),
        grid_spec=pltpu.PrefetchScalarGridSpec(
            num_scalar_prefetch=1,
            grid=(width // tile,),
            in_specs=in_specs,
            out_specs=out_specs,
        ),
        out_shape=out_shape,
        compiler_params=params(),
        cost_estimate=pl.CostEstimate(
            flops=2 * rows * units * n * width,
            bytes_accessed=2 * units * n * width + 6 * rows * width,
            transcendentals=0,
        ),
    )(jnp.stack(blocks), *args)


def on_device(
    n_ctx,
    n_smp,
    n_head,
    queries,
    prefix_cache,
    suffix_cache,
    suffix_length,
    cache_sample,
    residual,
    w_out,
    norm_gain,
    gate_matrix,
    w_up,
    w_down,
):
    ctx, smp, head = (lax.axis_index(name) for name in ("ctx", "smp", "head"))
    samples = queries.shape[0]
    own_rows = residual.shape[0]
    queries = queries.reshape(samples, -1)
    prefix = prefix_cache.reshape(2, prefix_cache.shape[1], -1)
    rows, span = suffix_cache.shape[1:3]
    suffix = suffix_cache.reshape(2, rows, span, -1)
    kv_heads = prefix.shape[2] // HD
    group = QUERY_HEADS // KEY_VALUE_HEADS
    heads = kv_heads * group // n_ctx

    row_ids = lax.dynamic_slice_in_dim(cache_sample, (ctx * n_smp + smp) * rows, rows, 0)
    local_ids = row_ids % samples
    ids = jnp.repeat(local_ids, heads)[:, None]
    one_hot = local_ids[:, None] == jnp.arange(samples, dtype=jnp.int32)[None, :]
    row_lengths = jnp.sum(jnp.where(one_hot, suffix_length[None, :], 0), axis=1)
    lens = jnp.repeat(row_lengths, heads)[None, :]

    order = sorted(range(1, n_ctx), key=lambda k: -min(k, n_ctx - k)) + [0]
    pieces = []
    for k in order:
        chunk = (ctx + k) % n_ctx
        kv = chunk * heads // group
        piece = attention_piece(chunk, kv, ids, lens, queries, prefix, suffix, heads)
        pieces.append(shift(piece, "ctx", n_ctx, k) if k else piece)
    attn = merge(pieces, heads)
    gathered = [attn] + [shift(attn, "smp", n_smp, k) for k in range(1, n_smp)]

    where = jnp.stack([ctx, smp, head])
    parts = project(where, gathered, w_out, n_ctx, n_head, own_rows)
    partial = exchange_heads(parts, n_head)
    halves = ring_sum(partial, n_ctx, own_rows)
    state, msg_a, msg_b = make_state(halves, partial[:own_rows], residual, norm_gain[None, :])

    got_a, got_b = ring_gather(msg_a, msg_b, n_ctx)
    left = jnp.concatenate(got_a, axis=0)
    right = jnp.concatenate(got_b, axis=0)
    full = jnp.concatenate([left, right], axis=1)
    full = jnp.concatenate(
        [full] + [shift(full, "head", n_head, b) for b in range(1, n_head)], axis=0
    )
    depth = gate_matrix.shape[0]
    square = full[:, depth:]
    squares = [square] + [shift(square, "smp", n_smp, k) for k in range(1, n_smp)]

    share = gate_matrix.shape[1] // n_smp
    splits = min(2, share // 128)
    units = share // splits
    received = [[] for _ in range(splits)]
    for k in range(1, n_smp):
        for q in range(splits):
            block = (smp + k) % n_smp * splits + q
            msg = gate_up(block, full, gate_matrix, w_up, units, BF16)
            received[q].append(shift(msg, "smp", n_smp, k))
    own = [
        gate_up(smp * splits + q, full, gate_matrix, w_up, units, F32) for q in range(splits)
    ]
    hidden, others = [], []
    for q in range(splits):
        hidden.append(activate(own[q], received[q], squares, units))
        others.append([shift(hidden[q], "smp", n_smp, k) for k in range(1, n_smp)])
    acc = down([smp * splits + q for q in range(splits)], hidden, w_down, None, n_head)
    blocks, xs = [], []
    for k in range(1, n_smp):
        for q in range(splits):
            blocks.append((smp + n_smp - k) % n_smp * splits + q)
            xs.append(others[q][k - 1])
    parts = down(blocks, xs, w_down, acc, n_head)
    partial = exchange_heads(parts, n_head)
    halves = ring_sum(partial, n_ctx, own_rows)
    total = (
        jnp.concatenate(halves, axis=1).astype(F32)
        + partial[:own_rows].astype(F32)
        + state.astype(F32)
    )
    return total.astype(BF16)


def solution(mesh):
    in_specs = (
        P(("group", "smp"), "head", None),
        P(None, ("group", "ctx"), "head", None),
        P(None, ("group", "ctx", "smp"), None, "head", None),
        P(("group", "smp")),
        P("group"),
        P(("group", "ctx", "head"), "smp"),
        P("head", "ctx", "smp"),
        P("smp"),
        P("smp", ("ctx", "head")),
        P("smp", ("ctx", "head")),
        P(("ctx", "head"), "smp"),
    )
    out_specs = P(("group", "ctx", "head"), "smp")
    body = functools.partial(
        on_device, mesh.shape["ctx"], mesh.shape["smp"], mesh.shape["head"]
    )
    return jax.shard_map(
        body, mesh=mesh, in_specs=in_specs, out_specs=out_specs, check_vma=False
    )
```

time: 361 us -> 206 us (0.57)
  waiting for transfers between devices: 216 us -> 64.3 us
  Pallas kernels: 0 us -> 87.1 us
  matrix products: 68.3 us -> 0 us
  starting transfers between devices: 11.5 us -> 41.4 us
  local copies, waits for them, and re-layouts: 24.4 us -> 5.67 us
  blocking collectives: 13.3 us -> 0 us
  between operations: 13.2 us -> 0.3 us
  other arithmetic: 12.6 us -> 6.12 us
    pallas_call x0 -> x15, Pallas kernels: none -> 87.1 us  [the longest x4 32.4 us: gate_up(): pl.pallas_call(gate_up_kernel, grid_spec=spec, out_shape=jax.ShapeDtypeSt...]
    reduce_scatter x2 -> x0, waiting for transfers between devices: 84.2 us -> none  [the longest x1 48.3 us: on_device(): lax.psum_scatter(jnp.dot(all_attn, proj_weight, preferred_element_type=jn...]
    dot_general x10 -> x0, matrix products: 68.3 us -> none  [the longest x1 12.6 us: on_device(): jnp.dot(activated, w_down, preferred_element_type=jnp.float32)]
    ppermute x0 -> x30, waiting for transfers between devices: none -> 64.3 us  [shift(): return lax.ppermute(x, axis, [(i, (i + k) % size) for i in range(size)])]
    psum x1 -> x0, waiting for transfers between devices: 57 us -> none  [on_device(): lax.psum(up_part.astype(jnp.bfloat16), 'smp').astype(jnp.float32)]
    all_to_all x2 -> x0, waiting for transfers between devices: 47.6 us -> none  [the longest x1 47.6 us: on_device(): lax.all_to_all(local_out.reshape(group_rows, 1, -1), 'ctx', split_axis=2,...]
    ppermute x0 -> x30, starting transfers between devices: none -> 41.4 us  [shift(): return lax.ppermute(x, axis, [(i, (i + k) % size) for i in range(size)])]
    all_gather x1 -> x0, waiting for transfers between devices: 27.4 us -> none  [on_device(): state = lax.all_gather(own_state, ('ctx', 'head'), axis=0, tiled=True)]
  transfers between devices with their start and end apart: 6 -> 30, of which waited for: 5 -> 21; matrix products, arithmetic and copies ran while one was open for 6% -> 0% of each run, Pallas kernels for 0% -> 26%
where the time goes in v1:
time: 206 us; the launch traced here: 205 us
  Pallas kernels  87.1 us (42%)
  waiting for transfers between devices  64.3 us (31%)
  starting transfers between devices  41.4 us (20%)
  other arithmetic  6.12 us (3%)
  local copies, waits for them, and re-layouts  5.67 us (3%)
    ppermute x30, waiting for transfers between devices, shift(): return lax.ppermute(x, axis, [(i, (i + k) % size) for i in range(size)])  64.3 us
    ppermute x30, starting transfers between devices, shift(): return lax.ppermute(x, axis, [(i, (i + k) % size) for i in range(size)])  41.4 us
    pallas_call x4, Pallas kernels, gate_up(): pl.pallas_call(gate_up_kernel, grid_spec=spec, out_shape=jax.ShapeDtypeSt...  32.4 us
    pallas_call x4, Pallas kernels, attention_piece(): pl.pallas_call(functools.partial(attention_kernel, heads), grid_spec=spec...  25.5 us
    pallas_call x2, Pallas kernels, down(): pl.pallas_call(functools.partial(down_kernel, n, acc is not None, n_head)...  16.8 us
    pallas_call x1, Pallas kernels, project(): pl.pallas_call(functools.partial(proj_kernel, n_ctx, n_head, own_rows, n_...  8.06 us
    unnamed x16, local copies, waits for them, and re-layouts  5.27 us
  transfers between devices with their start and end apart: 30, of which 21 were waited for; matrix products, arithmetic and copies ran while one was open for 0% of the time, Pallas kernels for 26%

profile of v1, /device:TPU:0, one launch (start us, length us, event | category | flops | bytes accessed | tf_op | source)
XLA Modules:
  0.0 204.8 jit_solution(7210568554412895052)
XLA Ops:
  4.9 6.8 %shard_map.109 = bf16[1056,128]{1,0:T(8,128)(2,1)} custom-call(s32[2]{0:T(128)S(1)} %pad_add_fusion.2.chunk_ref, s32[256,1]{1,0:T(8,128)S(1)} %broadcast_in_dim_reshape.8.ids_ref, s32[1,256]{1,0:T(1,128)S(1)} %broadcast_in_dim_reshape.7.lens_ref, bf16[128,4096]{1,0:T(8,128)(2,1)S(1)} %bitcast.27, bf16[2,1024,512]{2,1,0:T(8,128)(2,1)S(1)} %bitcast.19, ...), custom_call_target="tpu_custom_call" | custom-call | flops 2147483648 | bytes 5242880 | tf_op jit(solution)/shard_map/pallas_call | solution.py:145
  11.6 4.0 %collective-permute-start = (bf16[1056,128]{1,0:T(8,128)(2,1)}, bf16[1056,128]{1,0:T(8,128)(2,1)S(1)}, u32[]{:S(2)}, u32[]{:S(2)}) collective-permute-start(bf16[1056,128]{1,0:T(8,128)(2,1)} %shard_map.109), channel_id=1, source_target_pairs={{0,8},{4,12},{8,0},{12,4},{1,9},{5,13},{9,1},{13,5},{2,10},{6,14},... | collective-permute-start | bytes 811016 | tf_op jit(solution)/shard_map/ppermute | solution.py:44
  15.7 6.5 %shard_map.110 = bf16[1056,128]{1,0:T(8,128)(2,1)} custom-call(s32[2]{0:T(128)S(1)} %pad_add_fusion.3.chunk_ref, s32[256,1]{1,0:T(8,128)S(1)} %broadcast_in_dim_reshape.8.ids_ref, s32[1,256]{1,0:T(1,128)S(1)} %broadcast_in_dim_reshape.7.lens_ref, bf16[128,4096]{1,0:T(8,128)(2,1)S(1)} %bitcast.28, bf16[2,1024,512]{2,1,0:T(8,128)(2,1)S(1)} %bitcast.21, ...), custom_call_target="tpu_custom_call" | custom-call | flops 2147483648 | bytes 5242880 | tf_op jit(solution)/shard_map/pallas_call | solution.py:145
  23.9 6.5 %shard_map.111 = bf16[1056,128]{1,0:T(8,128)(2,1)} custom-call(s32[2]{0:T(128)S(1)} %pad_add_fusion.4.chunk_ref, s32[256,1]{1,0:T(8,128)S(1)} %broadcast_in_dim_reshape.8.ids_ref, s32[1,256]{1,0:T(1,128)S(1)} %broadcast_in_dim_reshape.7.lens_ref, bf16[128,4096]{1,0:T(8,128)(2,1)S(1)} %bitcast.29, bf16[2,1024,512]{2,1,0:T(8,128)(2,1)S(1)} %bitcast.23, ...), custom_call_target="tpu_custom_call" | custom-call | flops 2147483648 | bytes 5242880 | tf_op jit(solution)/shard_map/pallas_call | solution.py:145
  32.7 5.8 %shard_map.112.refs_3_ = bf16[1056,128]{1,0:T(8,128)(2,1)S(1)} custom-call(s32[2]{0:T(128)S(1)} %pad_add_fusion.5.chunk_ref, s32[256,1]{1,0:T(8,128)S(1)} %broadcast_in_dim_reshape.8.ids_ref, s32[1,256]{1,0:T(1,128)S(1)} %broadcast_in_dim_reshape.7.lens_ref, bf16[128,4096]{1,0:T(8,128)(2,1)S(1)} %bitcast.30, bf16[2,1024,512]{2,1,0:T(8,128)(2,1)S(1)} %bitcast.25, ...), custom_call_target="tpu_custom_call" | custom-call | flops 2147483648 | bytes 5242880 | tf_op jit(solution)/shard_map/pallas_call | solution.py:145
  42.8 6.1 %collective-permute-done.3.refs_1_ = bf16[128,1024]{1,0:T(8,128)(2,1)S(1)} collective-permute-done((bf16[128,1024]{1,0:T(8,128)(2,1)S(1)}, bf16[128,1024]{1,0:T(8,128)(2,1)S(1)}, u32[]{:S(2)}, u32[]{:S(2)}) %collective-permute-start.3) | collective-permute-done | bytes 262176 | tf_op jit(solution)/shard_map/ppermute | solution.py:44
  49.0 8.1 %shard_map.114 = (bf16[128,4096]{1,0:T(8,128)(2,1)S(1)}, bf16[128,4096]{1,0:T(8,128)(2,1)S(1)}) custom-call(s32[3]{0:T(128)S(1)} %pad_add_fusion.1.where_ref, bf16[128,1024]{1,0:T(8,128)(2,1)S(1)} %shard_map.113.refs_0_, bf16[128,1024]{1,0:T(8,128)(2,1)S(1)} %collective-permute-done.3.refs_1_, bf16[1,1024,4096]{2,1,0:T(8,128)(2,1)} %refs_2_.3), custom_call_target="tpu_custom_call" | custom-call | flops 2147483648 | bytes 11010048 | tf_op jit(solution)/shard_map/pallas_call | solution.py:239
  60.0 4.0 %collective-permute-start.8 = (bf16[32,2048]{1,0:T(8,128)(2,1)S(1)}, bf16[32,2048]{1,0:T(8,128)(2,1)S(1)}, u32[]{:S(2)}, u32[]{:S(2)}) collective-permute-start(bf16[32,2048]{1,0:T(8,128)(2,1)S(1)} %get-tuple-element.29), channel_id=1, source_target_pairs={{0,12},{4,0},{8,4},{12,8},{1,13},{5,1},{9,5},{13,9},{2,14},{6,2},{... | collective-permute-start | bytes 393224 | tf_op jit(solution)/shard_map/ppermute | solution.py:44
  64.0 3.9 %collective-permute-done.8 = bf16[32,2048]{1,0:T(8,128)(2,1)S(1)} collective-permute-done((bf16[32,2048]{1,0:T(8,128)(2,1)S(1)}, bf16[32,2048]{1,0:T(8,128)(2,1)S(1)}, u32[]{:S(2)}, u32[]{:S(2)}) %collective-permute-start.8) | collective-permute-done | bytes 131104 | tf_op jit(solution)/shard_map/ppermute | solution.py:44
  73.2 3.7 %collective-permute-done.9 = bf16[32,2048]{1,0:T(8,128)(2,1)S(1)} collective-permute-done((bf16[32,2048]{1,0:T(8,128)(2,1)S(1)}, bf16[32,2048]{1,0:T(8,128)(2,1)S(1)}, u32[]{:S(2)}, u32[]{:S(2)}) %collective-permute-start.9) | collective-permute-done | bytes 131104 | tf_op jit(solution)/shard_map/ppermute | solution.py:44
  85.0 3.3 %collective-permute-done.7.a_ref = bf16[32,2048]{1,0:T(8,128)(2,1)S(1)} collective-permute-done((bf16[32,2048]{1,0:T(8,128)(2,1)S(1)}, bf16[32,2048]{1,0:T(8,128)(2,1)S(1)}, u32[]{:S(2)}, u32[]{:S(2)}) %collective-permute-start.7) | collective-permute-done | bytes 131104 | tf_op jit(solution)/shard_map/ppermute | solution.py:44
  90.6 4.9 %collective-permute-done.14 = bf16[32,2176]{1,0:T(8,128)(2,1)S(1)} collective-permute-done((bf16[32,2176]{1,0:T(8,128)(2,1)S(1)}, bf16[32,2176]{1,0:T(8,128)(2,1)S(1)}, u32[]{:S(2)}, u32[]{:S(2)}) %collective-permute-start.14) | collective-permute-done | bytes 139296 | tf_op jit(solution)/shard_map/ppermute | solution.py:44
  97.5 4.7 %collective-permute-done.15 = bf16[32,2176]{1,0:T(8,128)(2,1)S(1)} collective-permute-done((bf16[32,2176]{1,0:T(8,128)(2,1)S(1)}, bf16[32,2176]{1,0:T(8,128)(2,1)S(1)}, u32[]{:S(2)}, u32[]{:S(2)}) %collective-permute-start.15) | collective-permute-done | bytes 139296 | tf_op jit(solution)/shard_map/ppermute | solution.py:44
  104.9 5.8 %collective-permute-done.13 = bf16[32,2048]{1,0:T(8,128)(2,1)S(1)} collective-permute-done((bf16[32,2048]{1,0:T(8,128)(2,1)S(1)}, bf16[32,2048]{1,0:T(8,128)(2,1)S(1)}, u32[]{:S(2)}, u32[]{:S(2)}) %collective-permute-start.13) | collective-permute-done | bytes 131104 | tf_op jit(solution)/shard_map/ppermute | solution.py:44
  116.0 8.1 %shard_map.117 = bf16[256,1024]{1,0:T(8,128)(2,1)S(1)} custom-call(s32[1]{0:T(128)} %bitcast.where_ref, bf16[256,4224]{1,0:T(8,128)(2,1)S(1)} %pad_maximum_fusion.x_ref, bf16[4096,2048]{1,0:T(8,128)(2,1)} %g_ref.7, bf16[4096,2048]{1,0:T(8,128)(2,1)} %u_ref.7), custom_call_target="tpu_custom_call" | custom-call | flops 2147483648 | bytes 11010048 | tf_op jit(solution)/shard_map/pallas_call | solution.py:361
  125.7 8.1 %shard_map.120 = bf16[256,1024]{1,0:T(8,128)(2,1)S(1)} custom-call(s32[1]{0:T(128)} %bitcast.1.where_ref, bf16[256,4224]{1,0:T(8,128)(2,1)S(1)} %pad_maximum_fusion.x_ref, bf16[4096,2048]{1,0:T(8,128)(2,1)} %g_ref.7, bf16[4096,2048]{1,0:T(8,128)(2,1)} %u_ref.7), custom_call_target="tpu_custom_call" | custom-call | flops 2147483648 | bytes 11010048 | tf_op jit(solution)/shard_map/pallas_call | solution.py:361
  136.0 8.1 %shard_map.119.refs_0_ = f32[256,1024]{1,0:T(8,128)S(1)} custom-call(s32[1]{0:T(128)} %bitcast.18.where_ref, bf16[256,4224]{1,0:T(8,128)(2,1)S(1)} %pad_maximum_fusion.x_ref, bf16[4096,2048]{1,0:T(8,128)(2,1)} %g_ref.7, bf16[4096,2048]{1,0:T(8,128)(2,1)} %u_ref.7), custom_call_target="tpu_custom_call" | custom-call | flops 2147483648 | bytes 11010048 | tf_op jit(solution)/shard_map/pallas_call | solution.py:361
  144.1 8.1 %shard_map.116.refs_0_ = f32[256,1024]{1,0:T(8,128)S(1)} custom-call(s32[1]{0:T(128)} %bitcast.2.where_ref, bf16[256,4224]{1,0:T(8,128)(2,1)S(1)} %pad_maximum_fusion.x_ref, bf16[4096,2048]{1,0:T(8,128)(2,1)} %g_ref.7, bf16[4096,2048]{1,0:T(8,128)(2,1)} %u_ref.7), custom_call_target="tpu_custom_call" | custom-call | flops 2147483648 | bytes 11010048 | tf_op jit(solution)/shard_map/pallas_call | solution.py:361
  157.2 8.0 %shard_map.122.refs_4_ = f32[256,4096]{1,0:T(8,128)S(1)} custom-call(s32[2]{0:T(128)S(1)} %pad_add_fusion.6.where_ref, bf16[256,512]{1,0:T(8,128)(2,1)S(1)} %shard_map.118.refs_0_, bf16[256,512]{1,0:T(8,128)(2,1)S(1)} %shard_map.121.refs_1_, bf16[2048,4096]{1,0:T(8,128)(2,1)} %refs_3_.3, bf16[2048,4096]{1,0:T(8,128)(2,1)} %refs_3_.3), custom_call_target="tpu_custom_call" | custom-call | flops 2147483648 | bytes 14680064 | tf_op jit(solution)/shard_map/pallas_call | solution.py:436
  167.2 8.7 %shard_map.123 = (bf16[128,4096]{1,0:T(8,128)(2,1)S(1)}, bf16[128,4096]{1,0:T(8,128)(2,1)S(1)}) custom-call(s32[2]{0:T(128)S(1)} %pad_add_fusion.where_ref, bf16[256,512]{1,0:T(8,128)(2,1)S(1)} %collective-permute-done.20.refs_0_, bf16[256,512]{1,0:T(8,128)(2,1)S(1)} %collective-permute-done.22.refs_1_, bf16[2048,4096]{1,0:T(8,128)(2,1)} %refs_3_.3, ...), custom_call_target="tpu_custom_call" | custom-call | flops 2147483648 | bytes 14680064 | tf_op jit(solution)/shard_map/pallas_call | solution.py:436
  179.1 3.8 %collective-permute-start.27 = (bf16[32,2048]{1,0:T(8,128)(2,1)S(1)}, bf16[32,2048]{1,0:T(8,128)(2,1)S(1)}, u32[]{:S(2)}, u32[]{:S(2)}) collective-permute-start(bf16[32,2048]{1,0:T(8,128)(2,1)S(1)} %get-tuple-element.24), channel_id=1, source_target_pairs={{0,12},{4,0},{8,4},{12,8},{1,13},{5,1},{9,5},{13,9},{2,14},{6,2},{... | collective-permute-start | bytes 393224 | tf_op jit(solution)/shard_map/ppermute | solution.py:44
  182.9 4.4 %collective-permute-done.24 = bf16[32,2048]{1,0:T(8,128)(2,1)S(1)} collective-permute-done((bf16[32,2048]{1,0:T(8,128)(2,1)S(1)}, bf16[32,2048]{1,0:T(8,128)(2,1)S(1)}, u32[]{:S(2)}, u32[]{:S(2)}) %collective-permute-start.24) | collective-permute-done | bytes 131104 | tf_op jit(solution)/shard_map/ppermute | solution.py:44
  191.4 3.7 %collective-permute-done.25 = bf16[32,2048]{1,0:T(8,128)(2,1)S(1)} collective-permute-done((bf16[32,2048]{1,0:T(8,128)(2,1)S(1)}, bf16[32,2048]{1,0:T(8,128)(2,1)S(1)}, u32[]{:S(2)}, u32[]{:S(2)}) %collective-permute-start.25) | collective-permute-done | bytes 131104 | tf_op jit(solution)/shard_map/ppermute | solution.py:44
  199.9 4.1 %collective-permute-done.26 = bf16[32,2048]{1,0:T(8,128)(2,1)S(1)} collective-permute-done((bf16[32,2048]{1,0:T(8,128)(2,1)S(1)}, bf16[32,2048]{1,0:T(8,128)(2,1)S(1)}, u32[]{:S(2)}, u32[]{:S(2)}) %collective-permute-start.26) | collective-permute-done | bytes 131104 | tf_op jit(solution)/shard_map/ppermute | solution.py:44
  (93 shorter events, 65.5 us)
Async XLA Ops:
  11.6 26.8 %collective-permute-start = (bf16[1056,128]{1,0:T(8,128)(2,1)}, bf16[1056,128]{1,0:T(8,128)(2,1)S(1)}, u32[]{:S(2)}, u32[]{:S(2)}) collective-permute-start(bf16[1056,128]{1,0:T(8,128)(2,1)} %shard_map.109), channel_id=1, source_target_pairs={{0,8},{4,12},{8,0},{12,4},{1,9},{5,13},{9,1},{13,5},{2,10},{6,14},... | collective-permute-start | bytes 811016 | tf_op jit(solution)/shard_map/ppermute | solution.py:44
  22.2 16.2 %collective-permute-start.1 = (bf16[1056,128]{1,0:T(8,128)(2,1)}, bf16[1056,128]{1,0:T(8,128)(2,1)}, u32[]{:S(2)}, u32[]{:S(2)}) collective-permute-start(bf16[1056,128]{1,0:T(8,128)(2,1)} %shard_map.110), channel_id=1, source_target_pairs={{0,4},{4,8},{8,12},{12,0},{1,5},{5,9},{9,13},{13,1},{2,6},{6,10},{... | collective-permute-start | bytes 811016 | tf_op jit(solution)/shard_map/ppermute | solution.py:44
  30.4 9.5 %collective-permute-start.2 = (bf16[1056,128]{1,0:T(8,128)(2,1)}, bf16[1056,128]{1,0:T(8,128)(2,1)}, u32[]{:S(2)}, u32[]{:S(2)}) collective-permute-start(bf16[1056,128]{1,0:T(8,128)(2,1)} %shard_map.111), channel_id=1, source_target_pairs={{0,12},{4,0},{8,4},{12,8},{1,13},{5,1},{9,5},{13,9},{2,14},{6,2},{... | collective-permute-start | bytes 811016 | tf_op jit(solution)/shard_map/ppermute | solution.py:44
  41.2 7.8 %collective-permute-start.3 = (bf16[128,1024]{1,0:T(8,128)(2,1)S(1)}, bf16[128,1024]{1,0:T(8,128)(2,1)S(1)}, u32[]{:S(2)}, u32[]{:S(2)}) collective-permute-start(bf16[128,1024]{1,0:T(8,128)(2,1)S(1)} %shard_map.113.refs_0_), channel_id=1, source_target_pairs={{0,2},{2,0},{1,3},{3,1},{4,6},{6,4},{5,7},{7,5},{8,10},{10,8},{9,1... | collective-permute-start | bytes 786440 | tf_op jit(solution)/shard_map/ppermute | solution.py:44
  60.0 7.9 %collective-permute-start.8 = (bf16[32,2048]{1,0:T(8,128)(2,1)S(1)}, bf16[32,2048]{1,0:T(8,128)(2,1)S(1)}, u32[]{:S(2)}, u32[]{:S(2)}) collective-permute-start(bf16[32,2048]{1,0:T(8,128)(2,1)S(1)} %get-tuple-element.29), channel_id=1, source_target_pairs={{0,12},{4,0},{8,4},{12,8},{1,13},{5,1},{9,5},{13,9},{2,14},{6,2},{... | collective-permute-start | bytes 393224 | tf_op jit(solution)/shard_map/ppermute | solution.py:44
  64.0 7.1 %collective-permute-start.5 = (bf16[32,2048]{1,0:T(8,128)(2,1)S(1)}, bf16[32,2048]{1,0:T(8,128)(2,1)S(1)}, u32[]{:S(2)}, u32[]{:S(2)}) collective-permute-start(bf16[32,2048]{1,0:T(8,128)(2,1)S(1)} %get-tuple-element.30), channel_id=1, source_target_pairs={{0,4},{4,8},{8,12},{12,0},{1,5},{5,9},{9,13},{13,1},{2,6},{6,10},{... | collective-permute-start | bytes 393224 | tf_op jit(solution)/shard_map/ppermute | solution.py:44
  72.9 6.8 %collective-permute-start.6 = (bf16[32,2048]{1,0:T(8,128)(2,1)S(1)}, bf16[32,2048]{1,0:T(8,128)(2,1)S(1)}, u32[]{:S(2)}, u32[]{:S(2)}) collective-permute-start(bf16[32,2048]{1,0:T(8,128)(2,1)S(1)} %get-tuple-element.28), channel_id=1, source_target_pairs={{0,4},{4,8},{8,12},{12,0},{1,5},{5,9},{9,13},{13,1},{2,6},{6,10},{... | collective-permute-start | bytes 393224 | tf_op jit(solution)/shard_map/ppermute | solution.py:44
  81.1 7.1 %collective-permute-start.7 = (bf16[32,2048]{1,0:T(8,128)(2,1)S(1)}, bf16[32,2048]{1,0:T(8,128)(2,1)S(1)}, u32[]{:S(2)}, u32[]{:S(2)}) collective-permute-start(bf16[32,2048]{1,0:T(8,128)(2,1)S(1)} %get-tuple-element.26), channel_id=1, source_target_pairs={{0,4},{4,8},{8,12},{12,0},{1,5},{5,9},{9,13},{13,1},{2,6},{6,10},{... | collective-permute-start | bytes 393224 | tf_op jit(solution)/shard_map/ppermute | solution.py:44
  88.5 7.0 %collective-permute-start.14 = (bf16[32,2176]{1,0:T(8,128)(2,1)S(1)}, bf16[32,2176]{1,0:T(8,128)(2,1)S(1)}, u32[]{:S(2)}, u32[]{:S(2)}) collective-permute-start(bf16[32,2176]{1,0:T(8,128)(2,1)S(1)} %get-tuple-element.15), channel_id=1, source_target_pairs={{0,12},{4,0},{8,4},{12,8},{1,13},{5,1},{9,5},{13,9},{2,14},{6,2},{... | collective-permute-start | bytes 417800 | tf_op jit(solution)/shard_map/ppermute | solution.py:44
  89.5 7.4 %collective-permute-start.11 = (bf16[32,2048]{1,0:T(8,128)(2,1)S(1)}, bf16[32,2048]{1,0:T(8,128)(2,1)S(1)}, u32[]{:S(2)}, u32[]{:S(2)}) collective-permute-start(bf16[32,2048]{1,0:T(8,128)(2,1)S(1)} %get-tuple-element.14), channel_id=1, source_target_pairs={{0,4},{4,8},{8,12},{12,0},{1,5},{5,9},{9,13},{13,1},{2,6},{6,10},{... | collective-permute-start | bytes 393224 | tf_op jit(solution)/shard_map/ppermute | solution.py:44
  97.0 6.9 %collective-permute-start.12 = (bf16[32,2048]{1,0:T(8,128)(2,1)S(1)}, bf16[32,2048]{1,0:T(8,128)(2,1)S(1)}, u32[]{:S(2)}, u32[]{:S(2)}) collective-permute-start(bf16[32,2048]{1,0:T(8,128)(2,1)S(1)} %collective-permute-done.11), channel_id=1, source_target_pairs={{0,4},{4,8},{8,12},{12,0},{1,5},{5,9},{9,13},{13,1},{2,6},{6,10},{... | collective-permute-start | bytes 393224 | tf_op jit(solution)/shard_map/ppermute | solution.py:44
  102.2 8.5 %collective-permute-start.16 = (bf16[32,2176]{1,0:T(8,128)(2,1)S(1)}, bf16[32,2176]{1,0:T(8,128)(2,1)S(1)}, u32[]{:S(2)}, u32[]{:S(2)}) collective-permute-start(bf16[32,2176]{1,0:T(8,128)(2,1)S(1)} %collective-permute-done.15), channel_id=1, source_target_pairs={{0,12},{4,0},{8,4},{12,8},{1,13},{5,1},{9,5},{13,9},{2,14},{6,2},{... | collective-permute-start | bytes 417800 | tf_op jit(solution)/shard_map/ppermute | solution.py:44
  103.8 6.8 %collective-permute-start.13 = (bf16[32,2048]{1,0:T(8,128)(2,1)S(1)}, bf16[32,2048]{1,0:T(8,128)(2,1)S(1)}, u32[]{:S(2)}, u32[]{:S(2)}) collective-permute-start(bf16[32,2048]{1,0:T(8,128)(2,1)S(1)} %collective-permute-done.12), channel_id=1, source_target_pairs={{0,4},{4,8},{8,12},{12,0},{1,5},{5,9},{9,13},{13,1},{2,6},{6,10},{... | collective-permute-start | bytes 393224 | tf_op jit(solution)/shard_map/ppermute | solution.py:44
  124.2 28.1 %collective-permute-start.18 = (bf16[256,1024]{1,0:T(8,128)(2,1)S(1)}, bf16[256,1024]{1,0:T(8,128)(2,1)}, u32[]{:S(2)}, u32[]{:S(2)}) collective-permute-start(bf16[256,1024]{1,0:T(8,128)(2,1)S(1)} %shard_map.117), channel_id=1, source_target_pairs={{0,2},{2,0},{1,3},{3,1},{4,6},{6,4},{5,7},{7,5},{8,10},{10,8},{9,1... | collective-permute-start | bytes 1572872 | tf_op jit(solution)/shard_map/ppermute | solution.py:44
  133.8 20.4 %collective-permute-start.21 = (bf16[256,1024]{1,0:T(8,128)(2,1)S(1)}, bf16[256,1024]{1,0:T(8,128)(2,1)}, u32[]{:S(2)}, u32[]{:S(2)}) collective-permute-start(bf16[256,1024]{1,0:T(8,128)(2,1)S(1)} %shard_map.120), channel_id=1, source_target_pairs={{0,2},{2,0},{1,3},{3,1},{4,6},{6,4},{5,7},{7,5},{8,10},{10,8},{9,1... | collective-permute-start | bytes 1572872 | tf_op jit(solution)/shard_map/ppermute | solution.py:44
  134.5 17.7 %collective-permute-start.19 = (bf16[256,128]{1,0:T(8,128)(2,1)S(1)}, bf16[256,128]{1,0:T(8,128)(2,1)S(1)}, u32[]{:S(2)}, u32[]{:S(2)}) collective-permute-start(bf16[256,128]{1,0:T(8,128)(2,1)S(1)} %slice.67.refs_2_), channel_id=1, source_target_pairs={{0,2},{2,0},{1,3},{3,1},{4,6},{6,4},{5,7},{7,5},{8,10},{10,8},{9,1... | collective-permute-start | bytes 196616 | tf_op jit(solution)/shard_map/ppermute | solution.py:44
  153.6 13.6 %collective-permute-start.20 = (bf16[256,512]{1,0:T(8,128)(2,1)S(1)}, bf16[256,512]{1,0:T(8,128)(2,1)S(1)}, u32[]{:S(2)}, u32[]{:S(2)}) collective-permute-start(bf16[256,512]{1,0:T(8,128)(2,1)S(1)} %shard_map.118.refs_0_), channel_id=1, source_target_pairs={{0,2},{2,0},{1,3},{3,1},{4,6},{6,4},{5,7},{7,5},{8,10},{10,8},{9,1... | collective-permute-start | bytes 786440 | tf_op jit(solution)/shard_map/ppermute | solution.py:44
  155.6 11.7 %collective-permute-start.22 = (bf16[256,512]{1,0:T(8,128)(2,1)S(1)}, bf16[256,512]{1,0:T(8,128)(2,1)S(1)}, u32[]{:S(2)}, u32[]{:S(2)}) collective-permute-start(bf16[256,512]{1,0:T(8,128)(2,1)S(1)} %shard_map.121.refs_1_), channel_id=1, source_target_pairs={{0,2},{2,0},{1,3},{3,1},{4,6},{6,4},{5,7},{7,5},{8,10},{10,8},{9,1... | collective-permute-start | bytes 786440 | tf_op jit(solution)/shard_map/ppermute | solution.py:44
  179.0 8.2 %collective-permute-start.24 = (bf16[32,2048]{1,0:T(8,128)(2,1)S(1)}, bf16[32,2048]{1,0:T(8,128)(2,1)S(1)}, u32[]{:S(2)}, u32[]{:S(2)}) collective-permute-start(bf16[32,2048]{1,0:T(8,128)(2,1)S(1)} %get-tuple-element.23), channel_id=1, source_target_pairs={{0,4},{4,8},{8,12},{12,0},{1,5},{5,9},{9,13},{13,1},{2,6},{6,10},{... | collective-permute-start | bytes 393224 | tf_op jit(solution)/shard_map/ppermute | solution.py:44
  179.1 8.4 %collective-permute-start.27 = (bf16[32,2048]{1,0:T(8,128)(2,1)S(1)}, bf16[32,2048]{1,0:T(8,128)(2,1)S(1)}, u32[]{:S(2)}, u32[]{:S(2)}) collective-permute-start(bf16[32,2048]{1,0:T(8,128)(2,1)S(1)} %get-tuple-element.24), channel_id=1, source_target_pairs={{0,12},{4,0},{8,4},{12,8},{1,13},{5,1},{9,5},{13,9},{2,14},{6,2},{... | collective-permute-start | bytes 393224 | tf_op jit(solution)/shard_map/ppermute | solution.py:44
  187.5 7.5 %collective-permute-start.25 = (bf16[32,2048]{1,0:T(8,128)(2,1)S(1)}, bf16[32,2048]{1,0:T(8,128)(2,1)S(1)}, u32[]{:S(2)}, u32[]{:S(2)}) collective-permute-start(bf16[32,2048]{1,0:T(8,128)(2,1)S(1)} %get-tuple-element.21), channel_id=1, source_target_pairs={{0,4},{4,8},{8,12},{12,0},{1,5},{5,9},{9,13},{13,1},{2,6},{6,10},{... | collective-permute-start | bytes 393224 | tf_op jit(solution)/shard_map/ppermute | solution.py:44
  188.9 7.1 %collective-permute-start.28 = (bf16[32,2048]{1,0:T(8,128)(2,1)S(1)}, bf16[32,2048]{1,0:T(8,128)(2,1)S(1)}, u32[]{:S(2)}, u32[]{:S(2)}) collective-permute-start(bf16[32,2048]{1,0:T(8,128)(2,1)S(1)} %get-tuple-element.22), channel_id=1, source_target_pairs={{0,12},{4,0},{8,4},{12,8},{1,13},{5,1},{9,5},{13,9},{2,14},{6,2},{... | collective-permute-start | bytes 393224 | tf_op jit(solution)/shard_map/ppermute | solution.py:44
  196.1 8.0 %collective-permute-start.26 = (bf16[32,2048]{1,0:T(8,128)(2,1)S(1)}, bf16[32,2048]{1,0:T(8,128)(2,1)S(1)}, u32[]{:S(2)}, u32[]{:S(2)}) collective-permute-start(bf16[32,2048]{1,0:T(8,128)(2,1)S(1)} %get-tuple-element.19), channel_id=1, source_target_pairs={{0,4},{4,8},{8,12},{12,0},{1,5},{5,9},{9,13},{13,1},{2,6},{6,10},{... | collective-permute-start | bytes 393224 | tf_op jit(solution)/shard_map/ppermute | solution.py:44
  197.0 7.0 %collective-permute-start.29 = (bf16[32,2048]{1,0:T(8,128)(2,1)S(1)}, bf16[32,2048]{1,0:T(8,128)(2,1)S(1)}, u32[]{:S(2)}, u32[]{:S(2)}) collective-permute-start(bf16[32,2048]{1,0:T(8,128)(2,1)S(1)} %get-tuple-element.20), channel_id=1, source_target_pairs={{0,12},{4,0},{8,4},{12,8},{1,13},{5,1},{9,5},{13,9},{2,14},{6,2},{... | collective-permute-start | bytes 393224 | tf_op jit(solution)/shard_map/ppermute | solution.py:44
  (14 other events, 110.1 us)
